TPU v7x, 256 devices: a whole 4x4x8 slice. The times are simulated.
256 devices in a mesh: cp: 32 (over y, x, core), hd: 8 (over z).
Axes of the slice: x: 4, y: 4, z: 8, core: 2. Of those that a mesh axis runs over, the one named last changes fastest.
Arguments:
- queries: bfloat16 [16384, 8192], P('cp', 'hd'), may hold values from -4.5 to 4.5
- keys: bfloat16 [16384, 1024], P(('cp', 'hd')), may hold values from -4.5 to 4.5
- values: bfloat16 [16384, 1024], P(('cp', 'hd')), may hold values from -6 to 6
- grads_out: bfloat16 [16384, 8192], P('cp', 'hd'), may hold values from -6 to 6
- doc_lengths: int32 [64], replicated, may hold values from 1 to 1536, 16384 in all
Outputs:
- attention_out: bfloat16 [16384, 8192], P('cp', 'hd')
- grad_queries: bfloat16 [16384, 8192], P('cp', 'hd')
- grad_keys: bfloat16 [16384, 1024], P(('cp', 'hd'))
- grad_values: bfloat16 [16384, 1024], P(('cp', 'hd'))
Inputs may be any that keep to these rules, and one draw needn't show every extreme that they name: `doc_lengths`: the lengths of the 64 documents in order; they sum to 16384 and the largest is exactly 1536.
All inputs are finite; a program needn't handle non-finite values.
Results may differ from a plain program's by a relative error of at most 0.025.
Values may be sent and summed in bfloat16 or wider, within the bound.
A program may use at most 128 MiB of HBM per device.

v0:
```python
import functools
import math

import jax
import jax.numpy as jnp
from jax import lax
from jax.experimental import pallas as pl
from jax.experimental.pallas import tpu as pltpu
from jax.sharding import PartitionSpec as P

HD = 128
REACH = 3
HALF = 256
ONES = 16
MASKED = -1e30
FLOOR = -5e29
MESH = pl.DeviceIdType.MESH
F32 = jnp.float32
BF16 = jnp.bfloat16


def dot(a, b):
    return jnp.dot(a, b, preferred_element_type=F32)


def key_range(distance, part, block):
    if distance == 0 and part == 0:
        return 0, HALF
    if distance == REACH and part == 1:
        return HALF, block
    return 0, block


def kernel(
    n_cp,
    n_hd,
    heads,
    block,
    doc_ref,
    k_ref,
    v_ref,
    q_ref,
    g_ref,
    out_ref,
    dq_ref,
    dk_ref,
    dv_ref,
    qs,
    gs,
    qt,
    gt,
    kv,
    kt,
    vt,
    first,
    weights,
    acc,
    top,
    total,
    delta,
    dqa,
    outb,
    dqb,
    part_sum,
    sent,
    came,
    final,
    load_sem,
    store_sem,
    local_sem,
    a_send,
    a_recv,
    x_send,
    x_recv,
    r_send,
    r_recv,
    f_send,
    f_recv,
):
    cp = lax.axis_index("cp")
    hd = lax.axis_index("hd")
    core = lax.rem(cp, 2)
    rows = block // n_hd
    scale = 1.0 / math.sqrt(HD)
    log_scale = scale * math.log2(math.e)

    def cp_at(step):
        return {"cp": lax.rem(cp + step + n_cp, n_cp)}

    def hd_at(step):
        return {"hd": lax.rem(hd + step, n_hd)}

    def columns(index):
        return pl.ds(pl.multiple_of(index * HD, HD), HD)

    def remote(src, dst, send_sem, recv_sem, device):
        return pltpu.make_async_remote_copy(
            src_ref=src,
            dst_ref=dst,
            send_sem=send_sem,
            recv_sem=recv_sem,
            device_id=device,
            device_id_type=MESH,
        )

    def load(which, h):
        source, target = ((q_ref, qs), (g_ref, gs))[which]
        return pltpu.make_async_copy(
            source.at[:, columns(h)], target.at[h], load_sem.at[which, h]
        )

    def store(which, h):
        source, target = ((outb, out_ref), (dqb, dq_ref))[which]
        return pltpu.make_async_copy(
            source.at[h], target.at[:, columns(h)], store_sem.at[which, h]
        )

    for which in range(2):
        for h in range(heads):
            load(which, h).start()
    barrier = pltpu.get_barrier_semaphore()
    for step in range(1, n_hd):
        pl.semaphore_signal(barrier, inc=1, device_id=hd_at(step), device_id_type=MESH)
    for step in (-2, -1, 1, 2):
        pl.semaphore_signal(barrier, inc=1, device_id=cp_at(step), device_id_type=MESH)
    pl.semaphore_wait(barrier, n_hd - 1 + 4)

    def exchange(which, step):
        source = (k_ref, v_ref)[which]
        peer = lax.rem(hd + step, n_hd)
        return remote(
            source.at[:, columns(peer)],
            kv.at[0, which, pl.ds(pl.multiple_of(hd * rows, rows), rows)],
            a_send.at[which, step],
            a_recv.at[which, step],
            {"hd": peer},
        )

    def exchange_own(which):
        source = (k_ref, v_ref)[which]
        return pltpu.make_async_copy(
            source.at[:, columns(hd)],
            kv.at[0, which, pl.ds(pl.multiple_of(hd * rows, rows), rows)],
            local_sem.at[which],
        )

    order = sorted(range(1, n_hd), key=lambda step: -min(step, n_hd - step))
    for which in range(2):
        for step in order:
            exchange(which, step).start()
        exchange_own(which).start()

    def ahead(which):
        return remote(
            kv.at[0, which], kv.at[2, which], x_send.at[0, which], x_recv.at[2, which], cp_at(2)
        )

    def beside_even(which):
        return remote(
            kv.at[0, which], kv.at[1, which], x_send.at[1, which], x_recv.at[1, which], cp_at(1)
        )

    def beside_odd(which):
        return remote(
            kv.at[2, which], kv.at[1, which], x_send.at[1, which], x_recv.at[1, which], cp_at(-1)
        )

    def onward(which):
        return remote(
            kv.at[2, which], kv.at[3, which], x_send.at[2, which], x_recv.at[3, which], cp_at(1)
        )

    position = cp * block + lax.broadcasted_iota(jnp.int32, (8, block), 1)

    def next_doc(i, carry):
        begin, start = carry
        begin = begin + doc_ref[i]
        return begin, jnp.where(position >= begin, begin, start)

    _, start = lax.fori_loop(
        0, doc_ref.shape[0], next_doc, (jnp.int32(0), jnp.zeros((8, block), jnp.int32))
    )
    first[...] = start - cp * block

    for which in range(2):
        for h in range(heads):
            load(which, h).wait()

    def turn_queries(h, _):
        qt[h] = qs[h].T
        gt[h] = gs[h].T
        return 0

    lax.fori_loop(0, heads, turn_queries, 0)
    for d in range(REACH + 1):
        vt[d, HD:, :] = jnp.ones((ONES, block), BF16)

    for which in range(2):
        for step in order:
            exchange(which, step).wait_recv()
        exchange_own(which).wait()
        ahead(which).start()

        @pl.when(core == 0)
        def _(which=which):
            beside_even(which).start()

    def turn_keys(d):
        kt[d] = kv[d, 0].T
        vt[d, :HD, :] = kv[d, 1].T

    def forward(d, h):
        for part in range(2):
            cols = slice(part * HALF, (part + 1) * HALF)
            low, high = key_range(d, part, block)
            scores = dot(kv[d, 0, low:high, :], qt[h, :, cols]) * log_scale
            shape = (high - low, HALF)
            key_pos = lax.broadcasted_iota(jnp.int32, shape, 0) + (low - d * block)
            allowed = key_pos >= first[0:1, cols]
            if d == 0:
                query_pos = lax.broadcasted_iota(jnp.int32, shape, 1) + part * HALF
                allowed = allowed & (key_pos <= query_pos)
            scores = jnp.where(allowed, scores, MASKED)
            peak = jnp.maximum(jnp.max(scores, axis=0, keepdims=True), FLOOR)
            tile = jnp.exp2(scores - peak).astype(BF16)
            weights[d, h, low:high, cols] = tile
            value = dot(vt[d, :, low:high], tile)
            acc[d, h, :, cols] = value[:HD]
            total[d, h, :, cols] = value[HD : HD + 8]
            top[d, h, :, cols] = jnp.broadcast_to(peak, (8, HALF))

    def finish(h):
        peaks = [top[d, h] for d in range(REACH + 1)]
        peak = functools.reduce(jnp.maximum, peaks)
        factors = [jnp.exp2(one - peak) for one in peaks]
        sums = functools.reduce(
            jnp.add, [factors[d] * total[d, h] for d in range(REACH + 1)]
        )
        inverse = 1.0 / sums
        value = None
        for d in range(REACH + 1):
            factor = factors[d] * inverse
            top[d, h] = factor
            term = acc[d, h] * factor[0:1]
            value = term if value is None else value + term
        rounded = value.astype(BF16)
        delta[h] = jnp.broadcast_to(
            jnp.sum(gt[h].astype(F32) * rounded.astype(F32), axis=0, keepdims=True), (8, block)
        )
        outb[h] = rounded.T
        store(0, h).start()

    def backward(d, h, first_term):
        for part in range(2):
            cols = slice(part * HALF, (part + 1) * HALF)
            low, high = key_range(d, part, block)
            prob = weights[d, h, low:high, cols].astype(F32) * top[d, h, 0:1, cols]
            dprob = dot(kv[d, 1, low:high, :], gt[h, :, cols])
            dscore = (prob * (dprob - delta[h, 0:1, cols])).astype(BF16)
            term = dot(kt[d, :, low:high], dscore)
            if first_term:
                dqa[h, :, cols] = term
            else:
                dqa[h, :, cols] += term
            part_sum[0, low:high, :] += dot(dscore, qs[h, cols, :])
            part_sum[1, low:high, :] += dot(prob.astype(BF16), gs[h, cols, :])

    def forward_all(d, last):
        turn_keys(d)

        def one(h, _):
            forward(d, h)
            if last:
                finish(h)
            return 0

        lax.fori_loop(0, heads, one, 0)

    forward_all(0, False)
    for which in range(2):
        ahead(which).wait_recv()
        onward(which).start()

        @pl.when(core == 1)
        def _(which=which):
            beside_odd(which).start()

    forward_all(2, False)
    for which in range(2):
        beside_even(which).wait_recv()
    forward_all(1, False)
    for which in range(2):
        onward(which).wait_recv()
    forward_all(3, True)

    def grads_back(which):
        return remote(
            sent.at[0, which], came.at[0, which], r_send.at[0, which], r_recv.at[0, which], cp_at(-1)
        )

    def grads_beside(which, step):
        return remote(
            sent.at[1, which],
            came.at[1, which],
            r_send.at[1, which],
            r_recv.at[1, which],
            cp_at(step),
        )

    def grads_chip(which):
        return remote(
            sent.at[2, which], came.at[2, which], r_send.at[2, which], r_recv.at[2, which], cp_at(-2)
        )

    def backward_all(d, first_term, last):
        part_sum[...] = jnp.zeros_like(part_sum)

        def one(h, _):
            backward(d, h, first_term)
            if last:
                dqb[h] = (dqa[h] * scale).astype(BF16).T
                store(1, h).start()
            return 0

        lax.fori_loop(0, heads, one, 0)

    factors = (scale, 1.0)
    backward_all(3, True, False)
    for which in range(2):
        sent[0, which] = (part_sum[which] * factors[which]).astype(BF16)
        grads_back(which).start()
    backward_all(1, False, False)
    for which in range(2):
        sent[1, which] = (part_sum[which] * factors[which]).astype(BF16)

        @pl.when(core == 0)
        def _(which=which):
            grads_beside(which, 1).start()

        @pl.when(core == 1)
        def _(which=which):
            grads_beside(which, -1).start()

    backward_all(2, False, False)
    for which in range(2):
        grads_back(which).wait_recv()
        chip_sum = part_sum[which] * factors[which] + came[0, which].astype(F32)

        @pl.when(core == 0)
        def _(which=which, chip_sum=chip_sum):
            sent[2, which] = chip_sum.astype(BF16)

        @pl.when(core == 1)
        def _(which=which, chip_sum=chip_sum):
            grads_beside(which, -1).wait_recv()
            sent[2, which] = (chip_sum + came[1, which].astype(F32)).astype(BF16)

        grads_chip(which).start()
    backward_all(0, False, True)

    def give(which, step):
        target = (dk_ref, dv_ref)[which]
        peer = lax.rem(hd + step, n_hd)
        return remote(
            final.at[which, pl.ds(pl.multiple_of(peer * rows, rows), rows)],
            target.at[:, columns(hd)],
            f_send.at[which, step],
            f_recv.at[which, step],
            {"hd": peer},
        )

    def give_own(which):
        target = (dk_ref, dv_ref)[which]
        return pltpu.make_async_copy(
            final.at[which, pl.ds(pl.multiple_of(hd * rows, rows), rows)],
            target.at[:, columns(hd)],
            local_sem.at[which],
        )

    for which in range(2):
        grads_chip(which).wait_recv()
        whole = part_sum[which] * factors[which] + came[2, which].astype(F32)

        @pl.when(core == 0)
        def _(which=which, whole=whole):
            grads_beside(which, 1).wait_recv()
            final[which] = (whole + came[1, which].astype(F32)).astype(BF16)

        @pl.when(core == 1)
        def _(which=which, whole=whole):
            final[which] = whole.astype(BF16)

        for step in order:
            give(which, step).start()
        give_own(which).start()

    for which in range(2):
        for step in order:
            give(which, step).wait_recv()
        give_own(which).wait()
    for which in range(2):
        for step in order:
            exchange(which, step).wait_send()
            give(which, step).wait_send()
        ahead(which).wait_send()
        beside_even(which).wait_send()
        onward(which).wait_send()
        grads_back(which).wait_send()
        grads_beside(which, 1).wait_send()
        grads_chip(which).wait_send()
        for h in range(heads):
            store(which, h).wait()


def on_device(n_cp, n_hd, queries, keys, values, grads_out, doc_lengths):
    block, width = queries.shape
    heads = width // HD
    blocks = REACH + 1
    vmem = pltpu.VMEM
    dma = pltpu.SemaphoreType.DMA
    anywhere = pl.BlockSpec(memory_space=pl.ANY)
    products = 6 * heads * 14 * HALF * HALF * HD * 2
    return pl.pallas_call(
        functools.partial(kernel, n_cp, n_hd, heads, block),
        out_shape=(
            jax.ShapeDtypeStruct(queries.shape, BF16),
            jax.ShapeDtypeStruct(queries.shape, BF16),
            jax.ShapeDtypeStruct(keys.shape, BF16),
            jax.ShapeDtypeStruct(values.shape, BF16),
        ),
        in_specs=[pl.BlockSpec(memory_space=pltpu.SMEM)] + [anywhere] * 4,
        out_specs=(anywhere,) * 4,
        scratch_shapes=[
            vmem((heads, block, HD), BF16),
            vmem((heads, block, HD), BF16),
            vmem((heads, HD, block), BF16),
            vmem((heads, HD, block), BF16),
            vmem((blocks, 2, block, HD), BF16),
            vmem((blocks, HD, block), BF16),
            vmem((blocks, HD + ONES, block), BF16),
            vmem((8, block), jnp.int32),
            vmem((blocks, heads, block, block), BF16),
            vmem((blocks, heads, HD, block), F32),
            vmem((blocks, heads, 8, block), F32),
            vmem((blocks, heads, 8, block), F32),
            vmem((heads, 8, block), F32),
            vmem((heads, HD, block), F32),
            vmem((heads, block, HD), BF16),
            vmem((heads, block, HD), BF16),
            vmem((2, block, HD), F32),
            vmem((3, 2, block, HD), BF16),
            vmem((3, 2, block, HD), BF16),
            vmem((2, block, HD), BF16),
            dma((2, heads)),
            dma((2, heads)),
            dma((2,)),
            dma((2, n_hd)),
            dma((2, n_hd)),
            dma((3, 2)),
            dma((4, 2)),
            dma((3, 2)),
            dma((3, 2)),
            dma((2, n_hd)),
            dma((2, n_hd)),
        ],
        compiler_params=pltpu.CompilerParams(
            collective_id=0, has_side_effects=True, vmem_limit_bytes=56 * 2**20
        ),
        cost_estimate=pl.CostEstimate(
            flops=products, bytes_accessed=8 * 2**20, transcendentals=products // (12 * HD)
        ),
    )(doc_lengths, keys, values, queries, grads_out)


def solution(mesh):
    in_specs = (P("cp", "hd"), P(("cp", "hd"), None), P(("cp", "hd"), None), P("cp", "hd"), P())
    out_specs = (P("cp", "hd"), P("cp", "hd"), P(("cp", "hd"), None), P(("cp", "hd"), None))
    return jax.shard_map(
        functools.partial(on_device, mesh.shape["cp"], mesh.shape["hd"]),
        mesh=mesh,
        in_specs=in_specs,
        out_specs=out_specs,
        check_vma=False,
    )
```

profile of v0, /device:TPU:30, one launch (start us, length us, event | category | flops | bytes accessed | tf_op | source)
XLA Modules:
  0.0 90.7 jit_solution(16370787900133720258)
XLA Ops:
  0.6 85.1 %shard_map.84 = (bf16[512,1024]{1,0:T(8,128)(2,1)}, bf16[512,1024]{1,0:T(8,128)(2,1)}, bf16[64,1024]{1,0:T(8,128)(2,1)}, bf16[64,1024]{1,0:T(8,128)(2,1)}) custom-call(s32[64]{0:T(128)} %doc_ref.1, bf16[64,1024]{1,0:T(8,128)(2,1)} %k_ref.1, bf16[64,1024]{1,0:T(8,128)(2,1)} %v_ref.1, bf16[512,1024]{1,0:T(8,128)(2,1)} %q_ref.1, bf16[512,1024]{1,0:T(8,128)(2,1)} %g_ref.1), custom_call_target="tpu_custom_call" | custom-call | flops 11274289152 | bytes 8388608 | tf_op jit(solution)/shard_map/pallas_call | solution.py:423
  85.7 0.0 copy-start
  85.7 2.4 %copy.13 = bf16[512,1024]{1,0:T(8,128)(2,1)} copy(bf16[512,1024]{1,0:T(8,128)(2,1)} %get-tuple-element.8) | data formatting | bytes 2097152
  88.1 0.0 copy-done
  88.1 0.0 copy-start.2
  88.1 1.0 %copy.14 = bf16[512,1024]{1,0:T(8,128)(2,1)} copy(bf16[512,1024]{1,0:T(8,128)(2,1)S(1)} %copy-done) | data formatting | bytes 2097152
  89.0 0.1 copy-done.2
  89.1 0.0 copy-start.1
  89.1 0.7 copy.15
  89.7 0.3 copy-done.1
  90.0 0.7 copy.16
Async XLA Ops:
  85.7 2.4 %copy-start = (bf16[512,1024]{1,0:T(8,128)(2,1)S(1)}, bf16[512,1024]{1,0:T(8,128)(2,1)}, u32[]{:S(2)}) copy-start(bf16[512,1024]{1,0:T(8,128)(2,1)} %get-tuple-element.9) | copy-start | bytes 3145732
  88.1 1.0 %copy-start.2 = (bf16[64,1024]{1,0:T(8,128)(2,1)S(1)}, bf16[64,1024]{1,0:T(8,128)(2,1)}, u32[]{:S(2)}) copy-start(bf16[64,1024]{1,0:T(8,128)(2,1)} %get-tuple-element.10) | copy-start | bytes 393220
  89.1 1.0 %copy-start.1 = (bf16[64,1024]{1,0:T(8,128)(2,1)S(1)}, bf16[64,1024]{1,0:T(8,128)(2,1)}, u32[]{:S(2)}) copy-start(bf16[64,1024]{1,0:T(8,128)(2,1)} %get-tuple-element.11) | copy-start | bytes 393220
where the time goes:
time: 92.3 us; the launch traced here: 90.7 us
  Pallas kernels  85.1 us (92%)
  local copies, waits for them, and re-layouts  4.98 us (5%)
    pallas_call x1, Pallas kernels, on_device(): pl.pallas_call(functools.partial(kernel, n_cp, n_hd, heads, block), out_s...  85.1 us
    unnamed x10, local copies, waits for them, and re-layouts  4.98 us

commit v1 on v0

--- a/solution.py
+++ b/solution.py
@@ -14,6 +14,7 @@
 ONES = 16
 MASKED = -1e30
 FLOOR = -5e29
+CEILING = 1e30
 MESH = pl.DeviceIdType.MESH
 F32 = jnp.float32
 BF16 = jnp.bfloat16
@@ -50,9 +51,12 @@
     qt,
     gt,
     kv,
+    ks,
     kt,
     vt,
     first,
+    begin,
+    bias,
     weights,
     acc,
     top,
@@ -171,29 +175,49 @@
         )
 
     position = cp * block + lax.broadcasted_iota(jnp.int32, (8, block), 1)
+    corner = jnp.full((ONES, block), cp * block, jnp.int32)
 
     def next_doc(i, carry):
-        begin, start = carry
-        begin = begin + doc_ref[i]
-        return begin, jnp.where(position >= begin, begin, start)
-
-    _, start = lax.fori_loop(
-        0, doc_ref.shape[0], next_doc, (jnp.int32(0), jnp.zeros((8, block), jnp.int32))
+        edge, start, start_first = carry
+        edge = edge + doc_ref[i]
+        return (
+            edge,
+            jnp.where(position >= edge, edge, start),
+            jnp.where(corner >= edge, edge, start_first),
+        )
+
+    _, start, start_first = lax.fori_loop(
+        0,
+        doc_ref.shape[0],
+        next_doc,
+        (jnp.int32(0), jnp.zeros((8, block), jnp.int32), jnp.zeros((ONES, block), jnp.int32)),
     )
     first[...] = start - cp * block
+    begin[...] = start_first - cp * block
+
+    def mask_rows(i, _):
+        rows_at = pl.ds(pl.multiple_of(i * 64, 64), 64)
+        key_pos = lax.broadcasted_iota(jnp.int32, (64, block), 0) + i * 64
+        query_pos = lax.broadcasted_iota(jnp.int32, (64, block), 1)
+        allowed = (key_pos >= first[0:1, :]) & (key_pos <= query_pos)
+        bias[rows_at, :] = jnp.where(allowed, 0.0, MASKED)
+        return 0
+
+    lax.fori_loop(0, block // 64, mask_rows, 0)
 
     for which in range(2):
         for h in range(heads):
             load(which, h).wait()
 
     def turn_queries(h, _):
-        qt[h] = qs[h].T
+        scaled = qs[h].astype(F32).T * log_scale
+        high = scaled.astype(BF16)
+        qt[h, :HD, :] = high
+        qt[h, HD:, :] = (scaled - high.astype(F32)).astype(BF16)
         gt[h] = gs[h].T
         return 0
 
     lax.fori_loop(0, heads, turn_queries, 0)
-    for d in range(REACH + 1):
-        vt[d, HD:, :] = jnp.ones((ONES, block), BF16)
 
     for which in range(2):
         for step in order:
@@ -205,29 +229,75 @@
         def _(which=which):
             beside_even(which).start()
 
+    def key_kept(d):
+        key_pos = lax.broadcasted_iota(jnp.int32, (block, HD), 0) - d * block
+        return key_pos >= begin[0:1, :HD]
+
     def turn_keys(d):
-        kt[d] = kv[d, 0].T
-        vt[d, :HD, :] = kv[d, 1].T
-
-    def forward(d, h):
-        for part in range(2):
-            cols = slice(part * HALF, (part + 1) * HALF)
+        keys, values = kv[d, 0], kv[d, 1]
+        if d == 0:
+            ks[d] = keys
+            kt[d] = keys.T
+            vt[d, :HD, :] = values.T
+            vt[d, HD:, :] = jnp.ones((ONES, block), BF16)
+        else:
+            kept = key_kept(d)
+            wide = keys.astype(F32)
+            ks[d] = jnp.where(kept, wide, wide[block - 1 :, :]).astype(BF16)
+            kt[d] = jnp.where(kept, wide, 0.0).astype(BF16).T
+            vt[d, :HD, :] = jnp.where(kept, values.astype(F32), 0.0).astype(BF16).T
+            key_pos = lax.broadcasted_iota(jnp.int32, (ONES, block), 1) - d * block
+            vt[d, HD:, :] = jnp.where(key_pos >= begin[...], 1.0, 0.0).astype(BF16)
+
+    items = [(h, part) for h in range(heads) for part in range(2)]
+
+    def cols_of(part):
+        return slice(part * HALF, (part + 1) * HALF)
+
+    def forward_all(d, last):
+        turn_keys(d)
+
+        def scores_of(h, part):
             low, high = key_range(d, part, block)
-            scores = dot(kv[d, 0, low:high, :], qt[h, :, cols]) * log_scale
-            shape = (high - low, HALF)
-            key_pos = lax.broadcasted_iota(jnp.int32, shape, 0) + (low - d * block)
-            allowed = key_pos >= first[0:1, cols]
+            keys = ks[d, low:high, :]
+            return dot(jnp.concatenate([keys, keys], axis=1), qt[h, :, cols_of(part)])
+
+        def softmax(h, part, scores):
+            cols = cols_of(part)
+            low, high = key_range(d, part, block)
             if d == 0:
-                query_pos = lax.broadcasted_iota(jnp.int32, shape, 1) + part * HALF
-                allowed = allowed & (key_pos <= query_pos)
-            scores = jnp.where(allowed, scores, MASKED)
-            peak = jnp.maximum(jnp.max(scores, axis=0, keepdims=True), FLOOR)
+                scores = scores + bias[low:high, cols]
+                peak = jnp.max(scores, axis=0, keepdims=True)
+                kept_peak = peak
+            else:
+                reached = first[0:1, cols] < (1 - d) * block
+                peak = jnp.max(scores, axis=0, keepdims=True)
+                kept_peak = jnp.where(reached, peak, FLOOR)
+                peak = jnp.where(reached, peak, CEILING)
             tile = jnp.exp2(scores - peak).astype(BF16)
             weights[d, h, low:high, cols] = tile
+            top[d, h, :, cols] = jnp.broadcast_to(kept_peak, (8, HALF))
+            return tile
+
+        def weighted(h, part, tile):
+            cols = cols_of(part)
+            low, high = key_range(d, part, block)
             value = dot(vt[d, :, low:high], tile)
             acc[d, h, :, cols] = value[:HD]
             total[d, h, :, cols] = value[HD : HD + 8]
-            top[d, h, :, cols] = jnp.broadcast_to(peak, (8, HALF))
+            if last and part == 1:
+                finish(h)
+
+        ready = [scores_of(*item) for item in items[:2]]
+        late = None
+        for i, item in enumerate(items):
+            if i + 2 < len(items):
+                ready.append(scores_of(*items[i + 2]))
+            tile = softmax(*item, ready.pop(0))
+            if late is not None:
+                weighted(*late)
+            late = (*item, tile)
+        weighted(*late)
 
     def finish(h):
         peaks = [top[d, h] for d in range(REACH + 1)]
@@ -250,31 +320,44 @@
         outb[h] = rounded.T
         store(0, h).start()
 
-    def backward(d, h, first_term):
-        for part in range(2):
-            cols = slice(part * HALF, (part + 1) * HALF)
+    def backward_all(d, first_term, last):
+        part_sum[...] = jnp.zeros_like(part_sum)
+
+        def dprob_of(h, part):
             low, high = key_range(d, part, block)
-            prob = weights[d, h, low:high, cols].astype(F32) * top[d, h, 0:1, cols]
-            dprob = dot(kv[d, 1, low:high, :], gt[h, :, cols])
-            dscore = (prob * (dprob - delta[h, 0:1, cols])).astype(BF16)
+            return dot(kv[d, 1, low:high, :], gt[h, :, cols_of(part)])
+
+        def products(h, part, prob, dscore):
+            cols = cols_of(part)
+            low, high = key_range(d, part, block)
             term = dot(kt[d, :, low:high], dscore)
             if first_term:
                 dqa[h, :, cols] = term
             else:
                 dqa[h, :, cols] += term
             part_sum[0, low:high, :] += dot(dscore, qs[h, cols, :])
-            part_sum[1, low:high, :] += dot(prob.astype(BF16), gs[h, cols, :])
-
-    def forward_all(d, last):
-        turn_keys(d)
-
-        def one(h, _):
-            forward(d, h)
-            if last:
-                finish(h)
-            return 0
-
-        lax.fori_loop(0, heads, one, 0)
+            part_sum[1, low:high, :] += dot(prob, gs[h, cols, :])
+            if last and part == 1:
+                dqb[h] = (dqa[h] * scale).astype(BF16).T
+                store(1, h).start()
+
+        ready = [dprob_of(*item) for item in items[:2]]
+        late = None
+        for i, (h, part) in enumerate(items):
+            if i + 2 < len(items):
+                ready.append(dprob_of(*items[i + 2]))
+            cols = cols_of(part)
+            low, high = key_range(d, part, block)
+            prob = weights[d, h, low:high, cols].astype(F32) * top[d, h, 0:1, cols]
+            dscore = (prob * (ready.pop(0) - delta[h, 0:1, cols])).astype(BF16)
+            if late is not None:
+                products(*late)
+            late = (h, part, prob.astype(BF16), dscore)
+        products(*late)
+
+    def block_grads(d, which):
+        grads = part_sum[which] * (scale, 1.0)[which]
+        return grads if d == 0 else jnp.where(key_kept(d), grads, 0.0)
 
     forward_all(0, False)
     for which in range(2):
@@ -312,26 +395,13 @@
             sent.at[2, which], came.at[2, which], r_send.at[2, which], r_recv.at[2, which], cp_at(-2)
         )
 
-    def backward_all(d, first_term, last):
-        part_sum[...] = jnp.zeros_like(part_sum)
-
-        def one(h, _):
-            backward(d, h, first_term)
-            if last:
-                dqb[h] = (dqa[h] * scale).astype(BF16).T
-                store(1, h).start()
-            return 0
-
-        lax.fori_loop(0, heads, one, 0)
-
-    factors = (scale, 1.0)
     backward_all(3, True, False)
     for which in range(2):
-        sent[0, which] = (part_sum[which] * factors[which]).astype(BF16)
+        sent[0, which] = block_grads(3, which).astype(BF16)
         grads_back(which).start()
     backward_all(1, False, False)
     for which in range(2):
-        sent[1, which] = (part_sum[which] * factors[which]).astype(BF16)
+        sent[1, which] = block_grads(1, which).astype(BF16)
 
         @pl.when(core == 0)
         def _(which=which):
@@ -344,7 +414,7 @@
     backward_all(2, False, False)
     for which in range(2):
         grads_back(which).wait_recv()
-        chip_sum = part_sum[which] * factors[which] + came[0, which].astype(F32)
+        chip_sum = block_grads(2, which) + came[0, which].astype(F32)
 
         @pl.when(core == 0)
         def _(which=which, chip_sum=chip_sum):
@@ -379,7 +449,7 @@
 
     for which in range(2):
         grads_chip(which).wait_recv()
-        whole = part_sum[which] * factors[which] + came[2, which].astype(F32)
+        whole = block_grads(0, which) + came[2, which].astype(F32)
 
         @pl.when(core == 0)
         def _(which=which, whole=whole):
@@ -412,6 +482,25 @@
             store(which, h).wait()
 
 
+def hand_over(*refs):
+    count = len(refs) // 2
+    sem = refs[-1]
+    copies = []
+    for i in range(count):
+        source, target = refs[i], refs[count + i]
+        parts = 4 if i < 2 else 1
+        rows = source.shape[0] // parts
+        for j in range(parts):
+            at = slice(j * rows, (j + 1) * rows)
+            copies.append(
+                pltpu.make_async_copy(source.at[at], target.at[at], sem.at[len(copies)])
+            )
+    for copy in copies:
+        copy.start()
+    for copy in copies:
+        copy.wait()
+
+
 def on_device(n_cp, n_hd, queries, keys, values, grads_out, doc_lengths):
     block, width = queries.shape
     heads = width // HD
@@ -420,7 +509,7 @@
     dma = pltpu.SemaphoreType.DMA
     anywhere = pl.BlockSpec(memory_space=pl.ANY)
     products = 6 * heads * 14 * HALF * HALF * HD * 2
-    return pl.pallas_call(
+    results = pl.pallas_call(
         functools.partial(kernel, n_cp, n_hd, heads, block),
         out_shape=(
             jax.ShapeDtypeStruct(queries.shape, BF16),
@@ -433,12 +522,15 @@
         scratch_shapes=[
             vmem((heads, block, HD), BF16),
             vmem((heads, block, HD), BF16),
-            vmem((heads, HD, block), BF16),
+            vmem((heads, 2 * HD, block), BF16),
             vmem((heads, HD, block), BF16),
             vmem((blocks, 2, block, HD), BF16),
+            vmem((blocks, block, HD), BF16),
             vmem((blocks, HD, block), BF16),
             vmem((blocks, HD + ONES, block), BF16),
             vmem((8, block), jnp.int32),
+            vmem((ONES, block), jnp.int32),
+            vmem((block, block), F32),
             vmem((blocks, heads, block, block), BF16),
             vmem((blocks, heads, HD, block), F32),
             vmem((blocks, heads, 8, block), F32),
@@ -471,6 +563,15 @@
         ),
     )(doc_lengths, keys, values, queries, grads_out)
 
+    return pl.pallas_call(
+        hand_over,
+        out_shape=tuple(jax.ShapeDtypeStruct(one.shape, one.dtype) for one in results),
+        in_specs=[anywhere] * 4,
+        out_specs=(anywhere,) * 4,
+        scratch_shapes=[dma((10,))],
+        compiler_params=pltpu.CompilerParams(vmem_limit_bytes=56 * 2**20),
+    )(*results)
+
 
 def solution(mesh):
     in_specs = (P("cp", "hd"), P(("cp", "hd"), None), P(("cp", "hd"), None), P("cp", "hd"), P())

time: 92.3 us -> 130 us (1.41); the launches traced: 90.7 us -> 130 us
  Pallas kernels: 85.1 us -> 129 us
  local copies, waits for them, and re-layouts: 4.98 us -> 0 us
    pallas_call x0 -> x1, Pallas kernels: none -> 72.7 us  [on_device(): pl.pallas_call(hand_over, out_shape=tuple((jax.ShapeDtypeStruct(one.shape...]
    pallas_call x1, Pallas kernels: 85.1 us -> 56.8 us  [on_device(): pl.pallas_call(functools.partial(kernel, n_cp, n_hd, heads, block), out_s...]
    unnamed x10 -> x0, local copies, waits for them, and re-layouts: 4.98 us -> none
where the time goes in v1:
time: 130 us
  Pallas kernels  129 us (99%)
    pallas_call x1, Pallas kernels, on_device(): pl.pallas_call(hand_over, out_shape=tuple((jax.ShapeDtypeStruct(one.shape...  72.7 us
    pallas_call x1, Pallas kernels, on_device(): pl.pallas_call(functools.partial(kernel, n_cp, n_hd, heads, block), out_s...  56.8 us

profile of v1, /device:TPU:30, one launch (start us, length us, event | category | flops | bytes accessed | tf_op | source)
XLA Modules:
  0.0 130.2 jit_solution(5041107115902696581)
XLA Ops:
  0.6 56.8 %shard_map.84 = (bf16[512,1024]{1,0:T(8,128)(2,1)}, bf16[512,1024]{1,0:T(8,128)(2,1)}, bf16[64,1024]{1,0:T(8,128)(2,1)}, bf16[64,1024]{1,0:T(8,128)(2,1)}) custom-call(s32[64]{0:T(128)} %doc_ref.1, bf16[64,1024]{1,0:T(8,128)(2,1)} %k_ref.1, bf16[64,1024]{1,0:T(8,128)(2,1)} %v_ref.1, bf16[512,1024]{1,0:T(8,128)(2,1)} %q_ref.1, bf16[512,1024]{1,0:T(8,128)(2,1)} %g_ref.1), custom_call_target="tpu_custom_call" | custom-call | flops 11274289152 | bytes 8388608 | tf_op jit(solution)/shard_map/pallas_call | solution.py:512
  57.4 72.7 %shard_map.85 = (bf16[512,1024]{1,0:T(8,128)(2,1)}, bf16[512,1024]{1,0:T(8,128)(2,1)}, bf16[64,1024]{1,0:T(8,128)(2,1)}, bf16[64,1024]{1,0:T(8,128)(2,1)}) custom-call(bf16[512,1024]{1,0:T(8,128)(2,1)} %get-tuple-element.8.refs_0_, bf16[512,1024]{1,0:T(8,128)(2,1)} %get-tuple-element.9.refs_1_, bf16[64,1024]{1,0:T(8,128)(2,1)} %get-tuple-element.10.refs_2_, ...), custom_call_target="tpu_custom_call" | custom-call | tf_op jit(solution)/shard_map/pallas_call | solution.py:566

commit v2 on v1

--- a/solution.py
+++ b/solution.py
@@ -62,10 +62,10 @@
     top,
     total,
     delta,
-    dqa,
     outb,
     dqb,
     part_sum,
+    held,
     sent,
     came,
     final,
@@ -154,10 +154,14 @@
             exchange(which, step).start()
         exchange_own(which).start()
 
-    def ahead(which):
-        return remote(
-            kv.at[0, which], kv.at[2, which], x_send.at[0, which], x_recv.at[2, which], cp_at(2)
-        )
+    def ahead(which, step=None):
+        part = kv.at[0, which]
+        target = kv.at[2, which]
+        if step is not None:
+            owner = lax.rem(hd - step + n_hd, n_hd)
+            at = pl.ds(pl.multiple_of(owner * rows, rows), rows)
+            part, target = part.at[at], target.at[at]
+        return remote(part, target, x_send.at[0, which], x_recv.at[2, which], cp_at(2))
 
     def beside_even(which):
         return remote(
@@ -219,33 +223,59 @@
 
     lax.fori_loop(0, heads, turn_queries, 0)
 
-    for which in range(2):
-        for step in order:
+    def arrive_own(which):
+        exchange_own(which).wait()
+        ahead(which, 0).start()
+        for step in reversed(order):
             exchange(which, step).wait_recv()
-        exchange_own(which).wait()
-        ahead(which).start()
+            ahead(which, step).start()
 
         @pl.when(core == 0)
-        def _(which=which):
+        def _():
             beside_even(which).start()
+
+    def arrive_two_back(which):
+        ahead(which).wait_recv()
+        onward(which).start()
+
+        @pl.when(core == 1)
+        def _():
+            beside_odd(which).start()
+
+    def arrive_one_back(which):
+        beside_even(which).wait_recv()
+
+    def arrive_three_back(which):
+        onward(which).wait_recv()
+
+    def key_rows(d, low=0, high=block):
+        begin_at = (REACH - d) * block + low
+        if not isinstance(d, int):
+            begin_at = pl.multiple_of(begin_at, HALF)
+        return pl.ds(begin_at, high - low)
 
     def key_kept(d):
         key_pos = lax.broadcasted_iota(jnp.int32, (block, HD), 0) - d * block
         return key_pos >= begin[0:1, :HD]
 
     def turn_keys(d):
-        keys, values = kv[d, 0], kv[d, 1]
+        keys = kv[d, 0]
         if d == 0:
             ks[d] = keys
-            kt[d] = keys.T
-            vt[d, :HD, :] = values.T
-            vt[d, HD:, :] = jnp.ones((ONES, block), BF16)
+            kt[:, key_rows(d)] = keys.T
         else:
             kept = key_kept(d)
             wide = keys.astype(F32)
             ks[d] = jnp.where(kept, wide, wide[block - 1 :, :]).astype(BF16)
-            kt[d] = jnp.where(kept, wide, 0.0).astype(BF16).T
-            vt[d, :HD, :] = jnp.where(kept, values.astype(F32), 0.0).astype(BF16).T
+            kt[:, key_rows(d)] = jnp.where(kept, wide, 0.0).astype(BF16).T
+
+    def turn_values(d):
+        values = kv[d, 1]
+        if d == 0:
+            vt[d, :HD, :] = values.T
+            vt[d, HD:, :] = jnp.ones((ONES, block), BF16)
+        else:
+            vt[d, :HD, :] = jnp.where(key_kept(d), values.astype(F32), 0.0).astype(BF16).T
             key_pos = lax.broadcasted_iota(jnp.int32, (ONES, block), 1) - d * block
             vt[d, HD:, :] = jnp.where(key_pos >= begin[...], 1.0, 0.0).astype(BF16)
 
@@ -254,7 +284,8 @@
     def cols_of(part):
         return slice(part * HALF, (part + 1) * HALF)
 
-    def forward_all(d, last):
+    def forward_all(d, arrive, last, values_last=False):
+        arrive(0)
         turn_keys(d)
 
         def scores_of(h, part):
@@ -275,7 +306,7 @@
                 kept_peak = jnp.where(reached, peak, FLOOR)
                 peak = jnp.where(reached, peak, CEILING)
             tile = jnp.exp2(scores - peak).astype(BF16)
-            weights[d, h, low:high, cols] = tile
+            weights[h, key_rows(d, low, high), cols] = tile
             top[d, h, :, cols] = jnp.broadcast_to(kept_peak, (8, HALF))
             return tile
 
@@ -294,10 +325,22 @@
             if i + 2 < len(items):
                 ready.append(scores_of(*items[i + 2]))
             tile = softmax(*item, ready.pop(0))
-            if late is not None:
+            if values_last:
+                continue
+            if late is None:
+                arrive(1)
+                turn_values(d)
+            else:
                 weighted(*late)
             late = (*item, tile)
-        weighted(*late)
+        if values_last:
+            arrive(1)
+            turn_values(d)
+            for h, part in items:
+                low, high = key_range(d, part, block)
+                weighted(h, part, weights[h, key_rows(d, low, high), cols_of(part)])
+        else:
+            weighted(*late)
 
     def finish(h):
         peaks = [top[d, h] for d in range(REACH + 1)]
@@ -320,36 +363,42 @@
         outb[h] = rounded.T
         store(0, h).start()
 
-    def backward_all(d, first_term, last):
+    def prob_of(d, like, h, part):
+        cols = cols_of(part)
+        low, high = key_range(like, part, block)
+        return weights[h, key_rows(d, low, high), cols].astype(F32) * top[d, h, 0:1, cols]
+
+    def add_values(d, like, h, part, prob):
+        low, high = key_range(like, part, block)
+        part_sum[1, low:high, :] += dot(prob, gs[h, cols_of(part), :])
+
+    def backward_all(d, like, halfway=None, values_first=False):
         part_sum[...] = jnp.zeros_like(part_sum)
+        if values_first:
+            for h, part in items:
+                add_values(d, like, h, part, prob_of(d, like, h, part).astype(BF16))
 
         def dprob_of(h, part):
-            low, high = key_range(d, part, block)
+            low, high = key_range(like, part, block)
             return dot(kv[d, 1, low:high, :], gt[h, :, cols_of(part)])
 
         def products(h, part, prob, dscore):
-            cols = cols_of(part)
-            low, high = key_range(d, part, block)
-            term = dot(kt[d, :, low:high], dscore)
-            if first_term:
-                dqa[h, :, cols] = term
-            else:
-                dqa[h, :, cols] += term
-            part_sum[0, low:high, :] += dot(dscore, qs[h, cols, :])
-            part_sum[1, low:high, :] += dot(prob, gs[h, cols, :])
-            if last and part == 1:
-                dqb[h] = (dqa[h] * scale).astype(BF16).T
-                store(1, h).start()
+            low, high = key_range(like, part, block)
+            part_sum[0, low:high, :] += dot(dscore, qs[h, cols_of(part), :])
+            if not values_first:
+                add_values(d, like, h, part, prob)
 
         ready = [dprob_of(*item) for item in items[:2]]
         late = None
         for i, (h, part) in enumerate(items):
+            if halfway is not None and i == heads:
+                halfway()
             if i + 2 < len(items):
                 ready.append(dprob_of(*items[i + 2]))
-            cols = cols_of(part)
-            low, high = key_range(d, part, block)
-            prob = weights[d, h, low:high, cols].astype(F32) * top[d, h, 0:1, cols]
-            dscore = (prob * (ready.pop(0) - delta[h, 0:1, cols])).astype(BF16)
+            prob = prob_of(d, like, h, part)
+            dscore = (prob * (ready.pop(0) - delta[h, 0:1, cols_of(part)])).astype(BF16)
+            low, high = key_range(like, part, block)
+            weights[h, key_rows(d, low, high), cols_of(part)] = dscore
             if late is not None:
                 products(*late)
             late = (h, part, prob.astype(BF16), dscore)
@@ -357,37 +406,25 @@
 
     def block_grads(d, which):
         grads = part_sum[which] * (scale, 1.0)[which]
-        return grads if d == 0 else jnp.where(key_kept(d), grads, 0.0)
-
-    forward_all(0, False)
-    for which in range(2):
-        ahead(which).wait_recv()
-        onward(which).start()
-
-        @pl.when(core == 1)
-        def _(which=which):
-            beside_odd(which).start()
-
-    forward_all(2, False)
-    for which in range(2):
-        beside_even(which).wait_recv()
-    forward_all(1, False)
-    for which in range(2):
-        onward(which).wait_recv()
-    forward_all(3, True)
+        return jnp.where(key_kept(d), grads, 0.0)
+
+    forward_all(0, arrive_own, False, True)
+    forward_all(2, arrive_two_back, False, True)
+    forward_all(1, arrive_one_back, False)
+    forward_all(3, arrive_three_back, True)
 
     def grads_back(which):
         return remote(
             sent.at[0, which], came.at[0, which], r_send.at[0, which], r_recv.at[0, which], cp_at(-1)
         )
 
-    def grads_beside(which, step):
+    def grads_beside(which):
         return remote(
             sent.at[1, which],
             came.at[1, which],
             r_send.at[1, which],
             r_recv.at[1, which],
-            cp_at(step),
+            cp_at(1 - 2 * core),
         )
 
     def grads_chip(which):
@@ -395,38 +432,55 @@
             sent.at[2, which], came.at[2, which], r_send.at[2, which], r_recv.at[2, which], cp_at(-2)
         )
 
-    backward_all(3, True, False)
-    for which in range(2):
+    backward_all(3, 3)
+    for which in (1, 0):
         sent[0, which] = block_grads(3, which).astype(BF16)
         grads_back(which).start()
-    backward_all(1, False, False)
-    for which in range(2):
-        sent[1, which] = block_grads(1, which).astype(BF16)
+
+    second = 1 + core
+    backward_all(second, 1)
+    for which in (1, 0):
+        grads = block_grads(second, which)
 
         @pl.when(core == 0)
-        def _(which=which):
-            grads_beside(which, 1).start()
+        def _(which=which, grads=grads):
+            sent[1, which] = grads.astype(BF16)
+            grads_beside(which).start()
 
         @pl.when(core == 1)
-        def _(which=which):
-            grads_beside(which, -1).start()
-
-    backward_all(2, False, False)
-    for which in range(2):
-        grads_back(which).wait_recv()
-        chip_sum = block_grads(2, which) + came[0, which].astype(F32)
+        def _(which=which, grads=grads):
+            held[which] = grads
+
+    third = 2 - core
+
+    def third_done(which):
+        grads = block_grads(third, which)
 
         @pl.when(core == 0)
-        def _(which=which, chip_sum=chip_sum):
-            sent[2, which] = chip_sum.astype(BF16)
+        def _():
+            grads_back(which).wait_recv()
+            sent[2, which] = (grads + came[0, which].astype(F32)).astype(BF16)
+            grads_chip(which).start()
 
         @pl.when(core == 1)
-        def _(which=which, chip_sum=chip_sum):
-            grads_beside(which, -1).wait_recv()
-            sent[2, which] = (chip_sum + came[1, which].astype(F32)).astype(BF16)
-
-        grads_chip(which).start()
-    backward_all(0, False, True)
+        def _():
+            sent[1, which] = grads.astype(BF16)
+            grads_beside(which).start()
+
+    def third_halfway():
+        @pl.when(core == 1)
+        def _():
+            for which in (1, 0):
+                grads_back(which).wait_recv()
+                grads_beside(which).wait_recv()
+                others = came[0, which].astype(F32) + came[1, which].astype(F32)
+                sent[2, which] = (held[which] + others).astype(BF16)
+                grads_chip(which).start()
+
+        third_done(1)
+
+    backward_all(third, 2, third_halfway, True)
+    third_done(0)
 
     def give(which, step):
         target = (dk_ref, dv_ref)[which]
@@ -447,22 +501,36 @@
             local_sem.at[which],
         )
 
-    for which in range(2):
+    def finish_own(which):
         grads_chip(which).wait_recv()
-        whole = block_grads(0, which) + came[2, which].astype(F32)
+        whole = part_sum[which] * (scale, 1.0)[which] + came[2, which].astype(F32)
 
         @pl.when(core == 0)
-        def _(which=which, whole=whole):
-            grads_beside(which, 1).wait_recv()
+        def _():
+            grads_beside(which).wait_recv()
             final[which] = (whole + came[1, which].astype(F32)).astype(BF16)
 
         @pl.when(core == 1)
-        def _(which=which, whole=whole):
+        def _():
             final[which] = whole.astype(BF16)
 
         for step in order:
             give(which, step).start()
         give_own(which).start()
+
+    def grad_queries(some):
+        for h in some:
+            for part in range(2):
+                reach = pl.ds(part * HALF, REACH * block + HALF)
+                term = dot(kt[:, reach], weights[h, reach, cols_of(part)]) * scale
+                dqb[h, cols_of(part), :] = term.astype(BF16).T
+            store(1, h).start()
+
+    backward_all(0, 0, lambda: finish_own(1), True)
+    early = heads // 4
+    grad_queries(range(early))
+    finish_own(0)
+    grad_queries(range(early, heads))
 
     for which in range(2):
         for step in order:
@@ -476,28 +544,32 @@
         beside_even(which).wait_send()
         onward(which).wait_send()
         grads_back(which).wait_send()
-        grads_beside(which, 1).wait_send()
+        grads_beside(which).wait_send()
         grads_chip(which).wait_send()
         for h in range(heads):
             store(which, h).wait()
 
 
-def hand_over(*refs):
-    count = len(refs) // 2
-    sem = refs[-1]
-    copies = []
-    for i in range(count):
-        source, target = refs[i], refs[count + i]
-        parts = 4 if i < 2 else 1
-        rows = source.shape[0] // parts
-        for j in range(parts):
-            at = slice(j * rows, (j + 1) * rows)
-            copies.append(
-                pltpu.make_async_copy(source.at[at], target.at[at], sem.at[len(copies)])
-            )
-    for copy in copies:
+def pieces(shape):
+    step = min(shape[0], 128)
+    return [slice(at, at + step) for at in range(0, shape[0], step)]
+
+
+def hand_over(count, *refs):
+    sources, targets, held = refs[:count], refs[count : 2 * count], refs[2 * count : 3 * count]
+    in_sem, out_sem = refs[3 * count :]
+    loads, stores = [], []
+    for source, target, hold in zip(sources, targets, held):
+        for at in pieces(source.shape):
+            i = len(loads)
+            loads.append(pltpu.make_async_copy(source.at[at], hold.at[at], in_sem.at[i]))
+            stores.append(pltpu.make_async_copy(hold.at[at], target.at[at], out_sem.at[i]))
+    for copy in loads:
         copy.start()
-    for copy in copies:
+    for load, store in zip(loads, stores):
+        load.wait()
+        store.start()
+    for copy in stores:
         copy.wait()
 
 
@@ -526,19 +598,19 @@
             vmem((heads, HD, block), BF16),
             vmem((blocks, 2, block, HD), BF16),
             vmem((blocks, block, HD), BF16),
-            vmem((blocks, HD, block), BF16),
+            vmem((HD, blocks * block), BF16),
             vmem((blocks, HD + ONES, block), BF16),
             vmem((8, block), jnp.int32),
             vmem((ONES, block), jnp.int32),
             vmem((block, block), F32),
-            vmem((blocks, heads, block, block), BF16),
+            vmem((heads, blocks * block, block), BF16),
             vmem((blocks, heads, HD, block), F32),
             vmem((blocks, heads, 8, block), F32),
             vmem((blocks, heads, 8, block), F32),
             vmem((heads, 8, block), F32),
-            vmem((heads, HD, block), F32),
             vmem((heads, block, HD), BF16),
             vmem((heads, block, HD), BF16),
+            vmem((2, block, HD), F32),
             vmem((2, block, HD), F32),
             vmem((3, 2, block, HD), BF16),
             vmem((3, 2, block, HD), BF16),
@@ -563,12 +635,14 @@
         ),
     )(doc_lengths, keys, values, queries, grads_out)
 
+    count = sum(len(pieces(one.shape)) for one in results)
     return pl.pallas_call(
-        hand_over,
+        functools.partial(hand_over, len(results)),
         out_shape=tuple(jax.ShapeDtypeStruct(one.shape, one.dtype) for one in results),
-        in_specs=[anywhere] * 4,
-        out_specs=(anywhere,) * 4,
-        scratch_shapes=[dma((10,))],
+        in_specs=[anywhere] * len(results),
+        out_specs=(anywhere,) * len(results),
+        scratch_shapes=[vmem(one.shape, one.dtype) for one in results]
+        + [dma((count,)), dma((count,))],
         compiler_params=pltpu.CompilerParams(vmem_limit_bytes=56 * 2**20),
     )(*results)
 

time: 130 us -> 57.8 us (0.44)
  Pallas kernels: 129 us -> 56.4 us
    pallas_call x1, Pallas kernels: 72.7 us -> 2.51 us  [on_device(): pl.pallas_call(functools.partial(hand_over, len(results)), out_shape=tupl...]
    pallas_call x1, Pallas kernels: 56.8 us -> 53.9 us  [on_device(): pl.pallas_call(functools.partial(kernel, n_cp, n_hd, heads, block), out_s...]
where the time goes in v2:
time: 57.8 us; the launch traced here: 57.2 us
  Pallas kernels  56.4 us (98%)
  between operations  0.82 us (1%)
    pallas_call x1, Pallas kernels, on_device(): pl.pallas_call(functools.partial(kernel, n_cp, n_hd, heads, block), out_s...  53.9 us
    pallas_call x1, Pallas kernels, on_device(): pl.pallas_call(functools.partial(hand_over, len(results)), out_shape=tupl...  2.51 us

profile of v2, /device:TPU:30, one launch (start us, length us, event | category | flops | bytes accessed | tf_op | source)
XLA Modules:
  0.0 57.2 jit_solution(2424300976667275053)
XLA Ops:
  0.6 53.9 %shard_map.84 = (bf16[512,1024]{1,0:T(8,128)(2,1)}, bf16[512,1024]{1,0:T(8,128)(2,1)}, bf16[64,1024]{1,0:T(8,128)(2,1)}, bf16[64,1024]{1,0:T(8,128)(2,1)}) custom-call(s32[64]{0:T(128)} %doc_ref.1, bf16[64,1024]{1,0:T(8,128)(2,1)} %k_ref.1, bf16[64,1024]{1,0:T(8,128)(2,1)} %v_ref.1, bf16[512,1024]{1,0:T(8,128)(2,1)} %q_ref.1, bf16[512,1024]{1,0:T(8,128)(2,1)} %g_ref.1), custom_call_target="tpu_custom_call" | custom-call | flops 11274289152 | bytes 8388608 | tf_op jit(solution)/shard_map/pallas_call | solution.py:584
  54.5 2.5 %shard_map.85 = (bf16[512,1024]{1,0:T(8,128)(2,1)}, bf16[512,1024]{1,0:T(8,128)(2,1)}, bf16[64,1024]{1,0:T(8,128)(2,1)}, bf16[64,1024]{1,0:T(8,128)(2,1)}) custom-call(bf16[512,1024]{1,0:T(8,128)(2,1)} %get-tuple-element.8.refs_0_, bf16[512,1024]{1,0:T(8,128)(2,1)} %get-tuple-element.9.refs_1_, bf16[64,1024]{1,0:T(8,128)(2,1)} %get-tuple-element.10.refs_2_, ...), custom_call_target="tpu_custom_call" | custom-call | tf_op jit(solution)/shard_map/pallas_call | solution.py:639

commit v3 on v2

--- a/solution.py
+++ b/solution.py
@@ -62,6 +62,8 @@
     top,
     total,
     delta,
+    own_dprob,
+    outt,
     outb,
     dqb,
     part_sum,
@@ -119,14 +121,14 @@
             source.at[h], target.at[:, columns(h)], store_sem.at[which, h]
         )
 
-    for which in range(2):
-        for h in range(heads):
-            load(which, h).start()
     barrier = pltpu.get_barrier_semaphore()
     for step in range(1, n_hd):
         pl.semaphore_signal(barrier, inc=1, device_id=hd_at(step), device_id_type=MESH)
     for step in (-2, -1, 1, 2):
         pl.semaphore_signal(barrier, inc=1, device_id=cp_at(step), device_id_type=MESH)
+    for which in range(2):
+        for h in range(heads):
+            load(which, h).start()
     pl.semaphore_wait(barrier, n_hd - 1 + 4)
 
     def exchange(which, step):
@@ -360,8 +362,7 @@
         delta[h] = jnp.broadcast_to(
             jnp.sum(gt[h].astype(F32) * rounded.astype(F32), axis=0, keepdims=True), (8, block)
         )
-        outb[h] = rounded.T
-        store(0, h).start()
+        outt[h] = rounded
 
     def prob_of(d, like, h, part):
         cols = cols_of(part)
@@ -379,6 +380,8 @@
                 add_values(d, like, h, part, prob_of(d, like, h, part).astype(BF16))
 
         def dprob_of(h, part):
+            if like == 0:
+                return None
             low, high = key_range(like, part, block)
             return dot(kv[d, 1, low:high, :], gt[h, :, cols_of(part)])
 
@@ -396,8 +399,11 @@
             if i + 2 < len(items):
                 ready.append(dprob_of(*items[i + 2]))
             prob = prob_of(d, like, h, part)
-            dscore = (prob * (ready.pop(0) - delta[h, 0:1, cols_of(part)])).astype(BF16)
             low, high = key_range(like, part, block)
+            dprob = ready.pop(0)
+            if dprob is None:
+                dprob = own_dprob[h, low:high, cols_of(part)]
+            dscore = (prob * (dprob - delta[h, 0:1, cols_of(part)])).astype(BF16)
             weights[h, key_rows(d, low, high), cols_of(part)] = dscore
             if late is not None:
                 products(*late)
@@ -409,6 +415,9 @@
         return jnp.where(key_kept(d), grads, 0.0)
 
     forward_all(0, arrive_own, False, True)
+    for h, part in items:
+        low, high = key_range(0, part, block)
+        own_dprob[h, low:high, cols_of(part)] = dot(kv[0, 1, low:high, :], gt[h, :, cols_of(part)])
     forward_all(2, arrive_two_back, False, True)
     forward_all(1, arrive_one_back, False)
     forward_all(3, arrive_three_back, True)
@@ -518,8 +527,10 @@
             give(which, step).start()
         give_own(which).start()
 
-    def grad_queries(some):
-        for h in some:
+    def grad_queries():
+        for h in range(heads):
+            outb[h] = outt[h].T
+            store(0, h).start()
             for part in range(2):
                 reach = pl.ds(part * HALF, REACH * block + HALF)
                 term = dot(kt[:, reach], weights[h, reach, cols_of(part)]) * scale
@@ -527,10 +538,8 @@
             store(1, h).start()
 
     backward_all(0, 0, lambda: finish_own(1), True)
-    early = heads // 4
-    grad_queries(range(early))
     finish_own(0)
-    grad_queries(range(early, heads))
+    grad_queries()
 
     for which in range(2):
         for step in order:
@@ -608,6 +617,8 @@
             vmem((blocks, heads, 8, block), F32),
             vmem((blocks, heads, 8, block), F32),
             vmem((heads, 8, block), F32),
+            vmem((heads, block, block), F32),
+            vmem((heads, HD, block), BF16),
             vmem((heads, block, HD), BF16),
             vmem((heads, block, HD), BF16),
             vmem((2, block, HD), F32),

time: 57.8 us -> 57.5 us (level)
  no operation moved by 1% of the time
where the time goes in v3:
time: 57.5 us; the launch traced here: 57.3 us
  Pallas kernels  56.5 us (98%)
  between operations  0.82 us (1%)
    pallas_call x1, Pallas kernels, on_device(): pl.pallas_call(functools.partial(kernel, n_cp, n_hd, heads, block), out_s...  54 us
    pallas_call x1, Pallas kernels, on_device(): pl.pallas_call(functools.partial(hand_over, len(results)), out_shape=tupl...  2.51 us

profile of v3, /device:TPU:30, one launch (start us, length us, event | category | flops | bytes accessed | tf_op | source)
XLA Modules:
  0.0 57.3 jit_solution(2436452852623969534)
XLA Ops:
  0.6 54.0 %shard_map.84 = (bf16[512,1024]{1,0:T(8,128)(2,1)}, bf16[512,1024]{1,0:T(8,128)(2,1)}, bf16[64,1024]{1,0:T(8,128)(2,1)}, bf16[64,1024]{1,0:T(8,128)(2,1)}) custom-call(s32[64]{0:T(128)} %doc_ref.1, bf16[64,1024]{1,0:T(8,128)(2,1)} %k_ref.1, bf16[64,1024]{1,0:T(8,128)(2,1)} %v_ref.1, bf16[512,1024]{1,0:T(8,128)(2,1)} %q_ref.1, bf16[512,1024]{1,0:T(8,128)(2,1)} %g_ref.1), custom_call_target="tpu_custom_call" | custom-call | flops 11274289152 | bytes 8388608 | tf_op jit(solution)/shard_map/pallas_call | solution.py:593
  54.6 2.5 %shard_map.85 = (bf16[512,1024]{1,0:T(8,128)(2,1)}, bf16[512,1024]{1,0:T(8,128)(2,1)}, bf16[64,1024]{1,0:T(8,128)(2,1)}, bf16[64,1024]{1,0:T(8,128)(2,1)}) custom-call(bf16[512,1024]{1,0:T(8,128)(2,1)} %get-tuple-element.8.refs_0_, bf16[512,1024]{1,0:T(8,128)(2,1)} %get-tuple-element.9.refs_1_, bf16[64,1024]{1,0:T(8,128)(2,1)} %get-tuple-element.10.refs_2_, ...), custom_call_target="tpu_custom_call" | custom-call | tf_op jit(solution)/shard_map/pallas_call | solution.py:650
